TPU v7x, 32 devices: a whole 2x2x4 slice. The times are simulated.
32 devices in a mesh: grp: 8 (over z, y), exp: 4 (over x, core).
Axes of the slice: x: 2, y: 2, z: 4, core: 2. Of those that a mesh axis runs over, the one named last changes fastest.
Arguments:
- tokens: bfloat16 [32, 192, 768], P(('grp', 'exp')), may hold values from -6 to 6
- seq_lengths: int32 [32], P('grp'), may hold values from 48 to 192, as said below
- deal_order: int32 [32], P('grp'), may hold values from 0 to 3, as said below
- expert_routes: int32 [32, 192, 2], P(('grp', 'exp')), may hold values from 0 to 3, as said below
- capacity_slots: int32 [32, 192, 2], P(('grp', 'exp')), may hold values from 0 to 143, as said below
- gate_weights: float32 [32, 192, 2], P(('grp', 'exp')), may hold values from 0.2 to 0.8
- cotangent: float32 [32, 192, 768], P(('grp', 'exp')), may hold values from -6 to 6
- projector: float32 [3, 768, 768], P(None, ('grp', 'exp')), may hold values from -0.3125 to 0.3125
- projector_mean: float32 [3, 768, 768], P(None, ('grp', 'exp')), may hold values from -256 to 256
- projector_square: float32 [3, 768, 768], P(None, ('grp', 'exp')), may hold values from 2211.84 to 8847.36
- collector: float32 [768, 768], P(('grp', 'exp')), may hold values from -0.875 to 0.875
- collector_first_moment: float32 [768, 768], P(('grp', 'exp')), may hold values from -96 to 96
- collector_second_moment: float32 [768, 768], P(('grp', 'exp')), may hold values from 245.76 to 983.04
- widener: float32 [2, 768, 2048], P(None, ('grp', 'exp')), may hold values from -0.21875 to 0.21875
- widener_mean: float32 [2, 768, 2048], P(None, ('grp', 'exp')), may hold values from -128 to 128
- widener_square: float32 [2, 768, 2048], P(None, ('grp', 'exp')), may hold values from 552.96 to 2211.84
- narrower: float32 [2048, 768], P(('grp', 'exp')), may hold values from -0.125 to 0.125
- narrower_mean: float32 [2048, 768], P(('grp', 'exp')), may hold values from -192 to 192
- narrower_square: float32 [2048, 768], P(('grp', 'exp')), may hold values from 983.04 to 3932.16
- norm_gains: float32 [2, 768], P(None, ('grp', 'exp')), may hold values from 0.5 to 1.5
- gains_mean: float32 [2, 768], P(None, ('grp', 'exp')), may hold values from -448 to 448
- gains_square: float32 [2, 768], P(None, ('grp', 'exp')), may hold values from 6144 to 24576
- expander: float32 [4, 2, 768, 2048], P('exp', None, 'grp'), may hold values from -0.21875 to 0.21875
- expander_mean: float32 [4, 2, 768, 2048], P('exp', None, 'grp'), may hold values from -48 to 48
- expander_square: float32 [4, 2, 768, 2048], P('exp', None, 'grp'), may hold values from 69.12 to 276.48
- reducer: float32 [4, 2048, 768], P('exp', 'grp'), may hold values from -0.125 to 0.125
- reducer_mean: float32 [4, 2048, 768], P('exp', 'grp'), may hold values from -80 to 80
- reducer_square: float32 [4, 2048, 768], P('exp', 'grp'), may hold values from 168.96 to 675.84
Outputs:
- block_output: float32 [32, 192, 768], P(('grp', 'exp'))
- input_grad: float32 [32, 192, 768], P(('grp', 'exp'))
- gate_grad: float32 [32, 192, 2], P(('grp', 'exp'))
- projector_moment: float32 [3, 768, 768], P(None, ('grp', 'exp'))
- projector_variance: float32 [3, 768, 768], P(None, ('grp', 'exp'))
- projector_weight: float32 [3, 768, 768], P(None, ('grp', 'exp'))
- collector_moment: float32 [768, 768], P(('grp', 'exp'))
- collector_variance: float32 [768, 768], P(('grp', 'exp'))
- collector_weight: float32 [768, 768], P(('grp', 'exp'))
- widener_moment: float32 [2, 768, 2048], P(None, ('grp', 'exp'))
- widener_variance: float32 [2, 768, 2048], P(None, ('grp', 'exp'))
- widener_weight: float32 [2, 768, 2048], P(None, ('grp', 'exp'))
- narrower_moment: float32 [2048, 768], P(('grp', 'exp'))
- narrower_variance: float32 [2048, 768], P(('grp', 'exp'))
- narrower_weight: float32 [2048, 768], P(('grp', 'exp'))
- gains_moment: float32 [2, 768], P(None, ('grp', 'exp'))
- gains_variance: float32 [2, 768], P(None, ('grp', 'exp'))
- gains_weight: float32 [2, 768], P(None, ('grp', 'exp'))
- expander_moment: float32 [4, 2, 768, 2048], P('exp', None, 'grp')
- expander_variance: float32 [4, 2, 768, 2048], P('exp', None, 'grp')
- expander_weight: float32 [4, 2, 768, 2048], P('exp', None, 'grp')
- reducer_moment: float32 [4, 2048, 768], P('exp', 'grp')
- reducer_variance: float32 [4, 2048, 768], P('exp', 'grp')
- reducer_weight: float32 [4, 2048, 768], P('exp', 'grp')
Inputs may be any that keep to these rules, and one draw needn't show every extreme that they name: `seq_lengths`: in each aligned block of 4 sequences one has length 192. `deal_order`: each aligned block of 4 entries is a permutation of 0 .. 3. `expert_routes`: A token's two experts differ. Within one slot no expert is named more than 144 times; in each aligned block of 4 slots some expert is named 144 times in every slot. Within one slot, the pairs (expert_routes, capacity_slots) are all different.
All inputs are finite; a program needn't handle non-finite values.
Results may differ from a plain program's by a relative error of at most 0.019.
The roundings to bfloat16 on the way count: a program that leaves them out, or rounds other values in their place, can miss the bound.
Values may be sent and summed in bfloat16 or wider, within the bound.
A program may use at most 256 MiB of HBM per device.

v0:
```python
import functools

import jax
import jax.numpy as jnp
import numpy as np
from jax import lax
from jax.experimental import pallas as pl
from jax.experimental.pallas import tpu as pltpu
from jax.sharding import PartitionSpec as P

HEAD_COUNT = 12
HEAD_FEATURES = 64
STEP = 5


def rms_factor(values):
    return lax.rsqrt(jnp.mean(values * values, axis=-1, keepdims=True) + 1e-06)


def rms_back(values, factor, upstream):
    return factor * (
        upstream - values * factor * factor * jnp.mean(upstream * values, axis=-1, keepdims=True)
    )


def rotary(length):
    positions = jnp.arange(length, dtype=jnp.int32).astype(jnp.float32)
    half = HEAD_FEATURES // 2
    freqs = jnp.exp(
        -jnp.log(10000.0) * jnp.arange(half, dtype=jnp.int32).astype(jnp.float32) / half
    )
    angles = positions[:, None] * freqs[None, :]
    return (jnp.cos(angles)[:, None, :], jnp.sin(angles)[:, None, :])


def rotate(values, cosines, sines):
    half = values.shape[-1] // 2
    first = values[..., :half]
    second = values[..., half:]
    return jnp.concatenate(
        [first * cosines - second * sines, second * cosines + first * sines], axis=-1
    )


def rotate_back(values, cosines, sines):
    half = values.shape[-1] // 2
    first = values[..., :half]
    second = values[..., half:]
    return jnp.concatenate(
        [first * cosines + second * sines, second * cosines - first * sines], axis=-1
    )


def silu_slope(values):
    sigmoid_of = jax.nn.sigmoid(values)
    return sigmoid_of * (1.0 + values * (1.0 - sigmoid_of))


def matmul(left, right):
    return jnp.dot(left, right, preferred_element_type=jnp.float32)


def outer_sum(left, right):
    return jnp.einsum("ld,lf->df", left, right, preferred_element_type=jnp.float32)


def adamw_update(weight, moment, variance, gradient, rate):
    moment_new = 0.5 * moment + 0.5 * gradient
    variance_new = 0.5 * variance + 0.5 * gradient * gradient
    correct = 1.0 - 0.5**STEP
    stepped = moment_new / correct / (jnp.sqrt(variance_new / correct) + 1e-08) + 0.1 * weight
    return (moment_new, variance_new, weight - rate * stepped)


def local_plain(
    tokens,
    seq_lengths,
    deal_order,
    expert_routes,
    capacity_slots,
    gate_weights,
    cotangent,
    projector,
    projector_mean,
    projector_square,
    collector,
    collector_first_moment,
    collector_second_moment,
    widener,
    widener_mean,
    widener_square,
    narrower,
    narrower_mean,
    narrower_square,
    norm_gains,
    gains_mean,
    gains_square,
    expander,
    expander_mean,
    expander_square,
    reducer,
    reducer_mean,
    reducer_square,
):
    members = lax.axis_size("exp")
    member = lax.axis_index("exp")
    length_seq = tokens.shape[1]
    width = tokens.shape[2]
    local_experts = expander.shape[0]
    experts_all = local_experts * members
    capacity = 3 * length_seq // experts_all
    member_ids = jnp.arange(members, dtype=jnp.int32)
    source = deal_order[member]
    home_slot = jnp.sum(jnp.where(deal_order == member, member_ids, 0))
    seq_length = seq_lengths[source]
    piece = lax.all_gather(tokens, "exp", axis=0, tiled=True)
    chosen = jnp.arange(piece.shape[0], dtype=jnp.int32) == source
    dealt = jnp.sum(
        jnp.where(chosen[:, None, None], piece, jnp.zeros_like(piece)), axis=0, keepdims=True
    )
    residual_flow = dealt[0].astype(jnp.float32)
    project_full, collect_full, widen_full, narrow_full, gains_full = (
        lax.all_gather(projector.astype(jnp.bfloat16), ("grp", "exp"), axis=1, tiled=True),
        lax.all_gather(collector.astype(jnp.bfloat16), ("grp", "exp"), axis=0, tiled=True),
        lax.all_gather(widener.astype(jnp.bfloat16), ("grp", "exp"), axis=1, tiled=True),
        lax.all_gather(narrower.astype(jnp.bfloat16), ("grp", "exp"), axis=0, tiled=True),
        lax.all_gather(norm_gains.astype(jnp.bfloat16), ("grp", "exp"), axis=1, tiled=True),
    )
    expand_full, reduce_full = (
        lax.all_gather(expander.astype(jnp.bfloat16), "grp", axis=2, tiled=True),
        lax.all_gather(reducer.astype(jnp.bfloat16), "grp", axis=1, tiled=True),
    )
    gains_used = gains_full.astype(jnp.float32)
    cosines, sines = rotary(length_seq)
    scale_one = rms_factor(residual_flow)
    normed_one = residual_flow * scale_one
    first_input = (normed_one * gains_used[0]).astype(jnp.bfloat16)
    query_raw = matmul(first_input, project_full[0]).reshape(length_seq, HEAD_COUNT, HEAD_FEATURES)
    key_raw = matmul(first_input, project_full[1]).reshape(length_seq, HEAD_COUNT, HEAD_FEATURES)
    value_raw = matmul(first_input, project_full[2]).reshape(length_seq, HEAD_COUNT, HEAD_FEATURES)
    query_rot = rotate(query_raw, cosines, sines).astype(jnp.bfloat16)
    key_rot = rotate(key_raw, cosines, sines).astype(jnp.bfloat16)
    value_low = value_raw.astype(jnp.bfloat16)
    rows_at = jnp.arange(length_seq, dtype=jnp.int32)[:, None]
    cols_at = jnp.arange(length_seq, dtype=jnp.int32)[None, :]
    allowed = ((cols_at <= rows_at) & (cols_at < seq_length))[None]
    scores = (
        jnp.einsum("qhd,khd->hqk", query_rot, key_rot, preferred_element_type=jnp.float32) * 0.125
    )
    masked = jnp.where(allowed, scores, -1e30)
    top = jnp.max(masked, axis=-1, keepdims=True)
    expo = jnp.exp(masked - top)
    total = jnp.sum(expo, axis=-1, keepdims=True)
    soft = expo / total
    logsum = top + jnp.log(total)
    mixed_output = (
        jnp.einsum(
            "hqk,khd->qhd", soft.astype(jnp.bfloat16), value_low, preferred_element_type=jnp.float32
        )
        .reshape(length_seq, width)
        .astype(jnp.bfloat16)
    )
    middle_state = residual_flow + matmul(mixed_output, collect_full)
    scale_two = rms_factor(middle_state)
    normed_two = middle_state * scale_two
    second_input = (normed_two * gains_used[1]).astype(jnp.bfloat16)
    gating_scores = matmul(second_input, widen_full[0])
    upward_rows = matmul(second_input, widen_full[1])
    hidden_state = (jax.nn.silu(gating_scores) * upward_rows).astype(jnp.bfloat16)
    dense_branch = matmul(hidden_state, narrow_full)
    flat = (expert_routes[0] * capacity + capacity_slots[0]).reshape(-1)
    spread = jnp.repeat(second_input, 2, axis=0)
    dispatch = jnp.zeros((experts_all * capacity, width), jnp.bfloat16).at[flat].set(spread)
    dispatch = dispatch.reshape(experts_all, capacity, width)
    rows = lax.all_to_all(dispatch, "exp", split_axis=0, concat_axis=0, tiled=True)
    count = rows.shape[1]
    grouped = rows.reshape(members, local_experts, count, width)
    gate_pre = jnp.einsum(
        "sekd,edf->sekf", grouped, expand_full[:, 0], preferred_element_type=jnp.float32
    )
    up_pre = jnp.einsum(
        "sekd,edf->sekf", grouped, expand_full[:, 1], preferred_element_type=jnp.float32
    )
    hidden_rows = (jax.nn.silu(gate_pre) * up_pre).astype(jnp.bfloat16)
    result = jnp.einsum(
        "sekf,efd->sekd", hidden_rows, reduce_full, preferred_element_type=jnp.float32
    )
    result = result.astype(jnp.bfloat16).reshape(members * local_experts, count, width)
    returned_rows = lax.all_to_all(result, "exp", split_axis=0, concat_axis=0, tiled=True)
    outcome = (
        returned_rows,
        rows,
        gate_pre.reshape(members * local_experts, count, -1),
        up_pre.reshape(members * local_experts, count, -1),
    )
    returned, received, gate_kept, up_kept = outcome
    picked = (
        returned.reshape(experts_all * capacity, width)[flat]
        .reshape(length_seq, 2, width)
        .astype(jnp.float32)
    )
    gate_local = gate_weights[0]
    mixture = jnp.sum(gate_local[..., None] * picked, axis=1)
    layer_output = middle_state + dense_branch + mixture
    valid = (jnp.arange(length_seq, dtype=jnp.int32) < seq_length).astype(jnp.float32)
    grad_out = cotangent[0] * valid[:, None]
    grad_low = grad_out.astype(jnp.bfloat16)
    narrow_grad = outer_sum(hidden_state, grad_low)
    hidden_grad = jnp.einsum("ld,fd->lf", grad_low, narrow_full, preferred_element_type=jnp.float32)
    gating_grad = (hidden_grad * upward_rows * silu_slope(gating_scores)).astype(jnp.bfloat16)
    upward_grad = (hidden_grad * jax.nn.silu(gating_scores)).astype(jnp.bfloat16)
    widen_grad = jnp.stack(
        [outer_sum(second_input, gating_grad), outer_sum(second_input, upward_grad)]
    )
    second_grad = jnp.einsum(
        "lf,df->ld", gating_grad, widen_full[0], preferred_element_type=jnp.float32
    ) + jnp.einsum("lf,df->ld", upward_grad, widen_full[1], preferred_element_type=jnp.float32)
    gate_grad_local = jnp.sum(grad_out[:, None, :] * picked, axis=-1)
    result_grad = (
        (gate_local[..., None] * grad_out[:, None, :])
        .astype(jnp.bfloat16)
        .reshape(2 * length_seq, width)
    )
    grad_send = jnp.zeros((experts_all * capacity, width), jnp.bfloat16).at[flat].set(result_grad)
    grad_recv = lax.all_to_all(
        grad_send.reshape(experts_all, capacity, width),
        "exp",
        split_axis=0,
        concat_axis=0,
        tiled=True,
    )
    grad_group = grad_recv.reshape(members, local_experts, capacity, width)
    rows_group = received.reshape(members, local_experts, capacity, width)
    gate_pre = gate_kept.reshape(members, local_experts, capacity, -1)
    up_pre = up_kept.reshape(members, local_experts, capacity, -1)
    hidden_rows = (jax.nn.silu(gate_pre) * up_pre).astype(jnp.bfloat16)
    reduce_grad = jnp.einsum(
        "sekf,sekd->efd", hidden_rows, grad_group, preferred_element_type=jnp.float32
    )
    hidden_rows_grad = jnp.einsum(
        "sekd,efd->sekf", grad_group, reduce_full, preferred_element_type=jnp.float32
    )
    gate_rows_grad = (hidden_rows_grad * up_pre * silu_slope(gate_pre)).astype(jnp.bfloat16)
    up_rows_grad = (hidden_rows_grad * jax.nn.silu(gate_pre)).astype(jnp.bfloat16)
    expand_grad = jnp.stack(
        [
            jnp.einsum(
                "sekd,sekf->edf", rows_group, gate_rows_grad, preferred_element_type=jnp.float32
            ),
            jnp.einsum(
                "sekd,sekf->edf", rows_group, up_rows_grad, preferred_element_type=jnp.float32
            ),
        ],
        axis=1,
    )
    row_grads = jnp.einsum(
        "sekf,edf->sekd", gate_rows_grad, expand_full[:, 0], preferred_element_type=jnp.float32
    ) + jnp.einsum(
        "sekf,edf->sekd", up_rows_grad, expand_full[:, 1], preferred_element_type=jnp.float32
    )
    row_grads = row_grads.astype(jnp.bfloat16).reshape(experts_all, capacity, width)
    came_back = lax.all_to_all(row_grads, "exp", split_axis=0, concat_axis=0, tiled=True).reshape(
        experts_all * capacity, width
    )
    second_grad = second_grad + jnp.sum(
        came_back[flat].reshape(length_seq, 2, width).astype(jnp.float32), axis=1
    )
    gains_grad_two = jnp.sum(second_grad * normed_two, axis=0)
    middle_grad = grad_out + rms_back(middle_state, scale_two, second_grad * gains_used[1])
    middle_low = middle_grad.astype(jnp.bfloat16)
    collect_grad = outer_sum(mixed_output, middle_low)
    mixed_grad = jnp.einsum(
        "ld,ed->le", middle_low, collect_full, preferred_element_type=jnp.float32
    )
    mixed_grad = mixed_grad.astype(jnp.bfloat16).reshape(length_seq, HEAD_COUNT, HEAD_FEATURES)
    scores_again = (
        jnp.einsum("qhd,khd->hqk", query_rot, key_rot, preferred_element_type=jnp.float32) * 0.125
    )
    soft_again = jnp.where(allowed, jnp.exp(scores_again - logsum), 0.0)
    value_grad = jnp.einsum(
        "hqk,qhd->khd",
        soft_again.astype(jnp.bfloat16),
        mixed_grad,
        preferred_element_type=jnp.float32,
    )
    soft_grad = jnp.einsum(
        "qhd,khd->hqk", mixed_grad, value_low, preferred_element_type=jnp.float32
    )
    score_grad = (
        soft_again * (soft_grad - jnp.sum(soft_again * soft_grad, axis=-1, keepdims=True))
    ).astype(jnp.bfloat16)
    query_grad = (
        jnp.einsum("hqk,khd->qhd", score_grad, key_rot, preferred_element_type=jnp.float32) * 0.125
    )
    key_grad = (
        jnp.einsum("hqk,qhd->khd", score_grad, query_rot, preferred_element_type=jnp.float32)
        * 0.125
    )
    query_back = (
        rotate_back(query_grad, cosines, sines).reshape(length_seq, width).astype(jnp.bfloat16)
    )
    key_back = rotate_back(key_grad, cosines, sines).reshape(length_seq, width).astype(jnp.bfloat16)
    value_back = value_grad.reshape(length_seq, width).astype(jnp.bfloat16)
    project_grad = jnp.stack(
        [
            outer_sum(first_input, query_back),
            outer_sum(first_input, key_back),
            outer_sum(first_input, value_back),
        ]
    )
    first_grad = (
        jnp.einsum("le,de->ld", query_back, project_full[0], preferred_element_type=jnp.float32)
        + jnp.einsum("le,de->ld", key_back, project_full[1], preferred_element_type=jnp.float32)
        + jnp.einsum("le,de->ld", value_back, project_full[2], preferred_element_type=jnp.float32)
    )
    gains_grad_one = jnp.sum(first_grad * normed_one, axis=0)
    stream_grad = middle_grad + rms_back(residual_flow, scale_one, first_grad * gains_used[0])
    gains_grad = jnp.stack([gains_grad_one, gains_grad_two])
    project_part, collect_part, widen_part, narrow_part, gains_part = (
        lax.psum_scatter(project_grad, ("grp", "exp"), scatter_dimension=1, tiled=True),
        lax.psum_scatter(collect_grad, ("grp", "exp"), scatter_dimension=0, tiled=True),
        lax.psum_scatter(widen_grad, ("grp", "exp"), scatter_dimension=1, tiled=True),
        lax.psum_scatter(narrow_grad, ("grp", "exp"), scatter_dimension=0, tiled=True),
        lax.psum_scatter(gains_grad, ("grp", "exp"), scatter_dimension=1, tiled=True),
    )
    expand_part, reduce_part = (
        lax.psum_scatter(
            expand_grad.astype(jnp.bfloat16), "grp", scatter_dimension=2, tiled=True
        ).astype(jnp.float32),
        lax.psum_scatter(
            reduce_grad.astype(jnp.bfloat16), "grp", scatter_dimension=1, tiled=True
        ).astype(jnp.float32),
    )
    empty = jnp.zeros((1, length_seq, width), jnp.float32)
    pieces = (
        lax.all_gather(layer_output[None].astype(jnp.bfloat16), "exp", axis=0, tiled=True).astype(
            jnp.float32
        ),
        lax.all_gather(stream_grad[None].astype(jnp.bfloat16), "exp", axis=0, tiled=True).astype(
            jnp.float32
        ),
    )
    chosen = (jnp.arange(pieces[0].shape[0], dtype=jnp.int32) == home_slot)[:, None, None]
    homed_output = empty + jnp.sum(jnp.where(chosen, pieces[0], 0.0), axis=0, keepdims=True)
    homed_grad = empty + jnp.sum(jnp.where(chosen, pieces[1], 0.0), axis=0, keepdims=True)
    project_new = adamw_update(projector, projector_mean, projector_square, project_part, 0.1)
    collect_new = adamw_update(
        collector, collector_first_moment, collector_second_moment, collect_part, 0.3
    )
    widening_updated = adamw_update(widener, widener_mean, widener_square, widen_part, 0.07)
    narrowing_updated = adamw_update(narrower, narrower_mean, narrower_square, narrow_part, 0.045)
    gains_updated = adamw_update(norm_gains, gains_mean, gains_square, gains_part, 0.2)
    expansion_updated = adamw_update(expander, expander_mean, expander_square, expand_part, 0.07)
    reduction_updated = adamw_update(reducer, reducer_mean, reducer_square, reduce_part, 0.045)
    return (
        homed_output,
        homed_grad,
        gate_grad_local[None],
        project_new[0],
        project_new[1],
        project_new[2],
        collect_new[0],
        collect_new[1],
        collect_new[2],
        widening_updated[0],
        widening_updated[1],
        widening_updated[2],
        narrowing_updated[0],
        narrowing_updated[1],
        narrowing_updated[2],
        gains_updated[0],
        gains_updated[1],
        gains_updated[2],
        expansion_updated[0],
        expansion_updated[1],
        expansion_updated[2],
        reduction_updated[0],
        reduction_updated[1],
        reduction_updated[2],
    )


MESH = pl.DeviceIdType.MESH
VMEM = pltpu.VMEM
LIMIT = 60 * 1024 * 1024


def ring_place(index, groups):
    row, side = lax.div(index, 2), lax.rem(index, 2)
    return (1 - side) * row + side * (groups - 1 - row)


def ring_member(place, groups):
    side = lax.div(place, groups // 2)
    return 2 * ((1 - side) * place + side * (groups - 1 - place)) + side


def remote(source, target, sends, arrivals, at, device):
    return pltpu.make_async_remote_copy(
        src_ref=source,
        dst_ref=target,
        send_sem=sends.at[at],
        recv_sem=arrivals.at[at],
        device_id=device,
        device_id_type=MESH,
    )


class Links:
    def __init__(self, sends, arrivals):
        self.sends, self.arrivals, self.count, self.started = sends, arrivals, 0, []

    def copy(self, source, target, device):
        made = remote(source, target, self.sends, self.arrivals, self.count, device)
        self.count += 1
        made.start()
        self.started.append(made)
        return made

    def finish(self):
        for made in self.started:
            made.wait_send()


class Places:
    def __init__(self, groups, members):
        self.groups, self.members = groups, members
        self.group = lax.axis_index("grp")
        self.member = lax.axis_index("exp")
        self.place = ring_place(self.group, groups)
        self.next = {"grp": self.owner(1)}
        self.back = {"grp": self.owner(-1)}
        half = members // 2
        self.far = lax.rem(self.member + half, members)
        self.near = self.member + 1 - 2 * lax.rem(self.member, 2)
        self.cross = lax.rem(self.near + half, members)
        self.peers = [lax.rem(self.member + step, members) for step in range(1, members)]

    def owner(self, offset):
        place = lax.rem(self.place + offset + 2 * self.groups, self.groups)
        return ring_member(place, self.groups)

    def enter(self):
        barrier = pltpu.get_barrier_semaphore()
        partners = [self.next, self.back] + [{"exp": peer} for peer in self.peers]
        for partner in partners:
            pl.semaphore_signal(barrier, inc=1, device_id=partner, device_id_type=MESH)
        pl.semaphore_wait(barrier, len(partners))


def rows(start, count, align=16):
    return pl.ds(pl.multiple_of(start, align), count)


def first_half(shape):
    return lax.rem(lax.broadcasted_iota(jnp.int32, shape, len(shape) - 1), 128) < 64


def turned(values):
    lanes = lax.broadcasted_iota(jnp.int32, values.shape, 1)
    return jnp.where(
        lax.rem(lanes, HEAD_FEATURES) < HEAD_FEATURES // 2,
        pltpu.roll(values, 128 - HEAD_FEATURES // 2, 1),
        pltpu.roll(values, HEAD_FEATURES // 2, 1),
    )


def nt(left, right):
    return lax.dot_general(
        left, right, (((1,), (1,)), ((), ())), preferred_element_type=jnp.float32
    )


def tn(left, right):
    return lax.dot_general(
        left, right, (((0,), (0,)), ((), ())), preferred_element_type=jnp.float32
    )


def sigmoid(values):
    return 1.0 / (1.0 + jnp.exp(-values))


def same(length):
    shape = (length, length)
    return lax.broadcasted_iota(jnp.int32, shape, 0) == lax.broadcasted_iota(jnp.int32, shape, 1)


def upright(line):
    return jnp.sum(jnp.where(same(line.shape[1]), line, 0.0), axis=1, keepdims=True)


def lying(column):
    return jnp.sum(jnp.where(same(column.shape[0]), column, 0.0), axis=0, keepdims=True)


def slot_of(deal_ref, member):
    for _ in range(11):
        member = deal_ref[member]
    return member


def dealt_lanes(values, piece, pieces):
    low_lanes = lax.broadcasted_iota(jnp.int32, (values.shape[0], 128), 1) < 64
    found = []
    span = 64 * pieces
    for start in range(0, values.shape[1], 2 * span):
        start = start + piece // 2 * 128
        one, two = values[:, start : start + 128], values[:, start + span : start + span + 128]
        if piece % 2:
            one = pltpu.roll(one, 64, 1)
        else:
            two = pltpu.roll(two, 64, 1)
        found.append(jnp.where(low_lanes, one, two))
    return jnp.concatenate(found, axis=1)


def joined_lanes(even, odd):
    low_lanes = lax.broadcasted_iota(jnp.int32, (even.shape[0], 128), 1) < 64
    found = []
    for start in range(0, even.shape[1], 128):
        one, two = even[:, start : start + 128], odd[:, start : start + 128]
        found.append(jnp.where(low_lanes, one, pltpu.roll(two, 64, 1)))
        found.append(jnp.where(low_lanes, pltpu.roll(one, 64, 1), two))
    return found


def gather_kernel(
    groups,
    members,
    length_ref,
    deal_ref,
    tokens,
    cotangent_in,
    routes,
    places,
    gates,
    norm_gains,
    projector,
    collector,
    widener_in,
    narrower_in,
    expander_in,
    reducer_in,
    cos_ref,
    sin_ref,
    wide_grads,
    down_grads,
    wide_first,
    down_first,
    attend_out,
    grads_out,
    saved_out,
    middle_out,
    soft_out,
    result_out,
    back_out,
    gains_full,
    gate_ref,
    cotangent,
    widener,
    narrower,
    expander,
    reducer,
    result_ref,
    back_ref,
    grads_home,
    attend_full,
    grads_all,
    saved,
    middle_ref,
    soft_ref,
    second_all,
    meta_send,
    meta_all,
    attend_send,
    attend_recv,
    widen_send,
    widen_recv,
    gains,
    gain_recv,
    gain_ring,
    wide_full,
    down_full,
    wide_own,
    down_own,
    inputs_ref,
    inputs_turned,
    dense_out,
    dense_back,
    rows_in,
    rows_turned,
    rows_grad,
    rows_out,
    rows_back,
    sends,
    arrivals,
    ring_sends,
    ring_arrivals,
    first_sends,
    first_arrivals,
    local_sems,
):
    at = Places(groups, members)
    links = Links(sends, arrivals)
    chunks, low = down_own.shape[:2]
    loads = {}
    for name, source, target in (
        ("expander", expander_in, expander),
        ("reducer", reducer_in, reducer),
        ("widener", widener_in, widener),
        ("narrower", narrower_in, narrower),
        ("cotangent", cotangent_in, cotangent),
    ):
        made = pltpu.make_async_copy(source, target, local_sems.at[2 * chunks + len(loads)])
        made.start(priority=1)
        loads[name] = made
    at.enter()
    me, steps = at.member, groups - 1
    share, width = projector.shape[1:]
    block = share * members
    length = tokens.shape[0]
    capacity = rows_in.shape[0] // members

    def ring_copy(chunk, step, side, piece):
        owner = at.owner(-step if side == 0 else step)
        if piece == 0:
            spot = wide_full.at[chunk, side, rows(owner * block, block), :]
            origin = wide_own.at[chunk, side]
        else:
            spot = down_full.at[chunk, rows(owner * low + side * (low // 2), low // 2), :]
            origin = down_own.at[chunk, pl.ds(side * (low // 2), low // 2), :]
        place = (chunk * steps + step) * 4 + side * 2 + piece
        return remote(
            spot if step else origin,
            spot,
            ring_sends,
            ring_arrivals,
            place,
            (at.next, at.back)[side],
        )

    def ring_step(chunk, step):
        for piece in range(2):
            for side in range(2):
                if step:
                    ring_copy(chunk, step - 1, side, piece).wait_recv()
                if step < steps:
                    ring_copy(chunk, step, side, piece).start()

    def tick(count):
        for chunk in range(chunks):
            if 0 <= count - 2 * chunk <= steps:
                ring_step(chunk, count - 2 * chunk)

    attend_send[0:3] = projector[...]
    attend_send[3] = collector[...]
    gains[...] = jnp.zeros_like(gains)
    gains[0:2, 0 : norm_gains.shape[1]] = norm_gains[...]
    gains[...] = pltpu.roll(gains[...], (at.group * members + me) * norm_gains.shape[1], 1)
    first_moves = [
        [
            links.copy(attend_send.at[peer], attend_recv.at[me], {"exp": peer}),
            links.copy(gains, gain_recv.at[me], {"exp": peer}),
        ]
        for peer in at.peers
    ]
    gain_recv[me] = gains[...]
    attend_recv[me] = attend_send[me]
    loads["widener"].wait()
    for matrix in range(2):
        for member in range(members):
            widen_send[member, matrix] = dealt_lanes(widener[matrix], member, members)
    widen_moves = [
        links.copy(widen_send.at[peer], widen_recv.at[me], {"exp": peer}) for peer in at.peers
    ]
    widen_recv[me] = widen_send[me]

    def stage(chunk):
        if chunk == 1:
            for matrix in range(2):
                wide_own[1, matrix] = jnp.concatenate(
                    [widen_recv[member, matrix] for member in range(members)], axis=0
                ).astype(jnp.bfloat16)
            down_own[1] = narrower[...].astype(jnp.bfloat16)
        else:
            index = max(chunk - 1, 0)
            for matrix in range(2):
                wide_own[chunk, matrix] = dealt_lanes(
                    expander[matrix], index, chunks - 1
                ).astype(jnp.bfloat16)
            down_own[chunk] = reducer[index * low : (index + 1) * low, :].astype(jnp.bfloat16)
        for side in range(2):
            wide_full[chunk, side, rows(at.group * block, block), :] = wide_own[chunk, side]
        down_full[chunk, rows(at.group * low, low), :] = down_own[chunk]

    loads["expander"].wait()
    loads["reducer"].wait()
    stage(0)
    tick(0)
    for moves in first_moves:
        for move in moves:
            move.wait_recv()
    attend_full[me, rows(at.group * block, block), :] = (
        attend_recv[...].reshape(block, width).astype(jnp.bfloat16)
    )
    total_gain = gain_recv[0]
    for member in range(1, members):
        total_gain = total_gain + gain_recv[member]
    gain_ring[at.group] = total_gain

    reach = (groups // 2, groups - 1 - groups // 2)

    def unit(owner, matrix):
        return attend_full.at[matrix, rows(owner * block, block), :]

    def across(owner):
        spot = unit(owner, me)
        return (links.copy(spot, spot, {"exp": at.far}), links.copy(spot, spot, {"exp": at.near}))

    crossed, passed, owners_seen = [], [], []

    def onward():
        spot = unit(owners_seen[len(passed)], at.far)
        crossed[len(passed)][0].wait_recv()
        passed.append(links.copy(spot, spot, {"exp": at.near}))

    ring = {}
    for step in range(reach[0] + 1):
        fresh = []
        for side, target in enumerate((at.next, at.back)):
            if step > reach[side]:
                continue
            owner = at.owner(-step if side == 0 else step)
            if step:
                for move in ring[step - 1, side]:
                    move.wait_recv()
            if step < reach[side]:
                spot, line = unit(owner, me), gain_ring.at[owner]
                ring[step, side] = (
                    links.copy(spot, spot, target),
                    links.copy(line, line, target),
                )
            if step or side == 0:
                fresh.append(owner)
        waiting = len(owners_seen) - len(passed)
        for owner in fresh:
            owners_seen.append(owner)
            crossed.append(across(owner))
        for _ in range(waiting):
            onward()
        if step == 1:
            for move in widen_moves:
                move.wait_recv()
            loads["narrower"].wait()
            for chunk in range(1, chunks):
                stage(chunk)
        if step:
            tick(step)
    outgoing = []

    def hand_out(source, target):
        made = pltpu.make_async_copy(
            source, target, local_sems.at[2 * chunks + len(loads) + len(outgoing)]
        )
        made.start(priority=1)
        outgoing.append(made)

    loads["cotangent"].wait()
    valid = lax.broadcasted_iota(jnp.int32, (length, 1), 0) < length_ref[deal_ref[me]]
    grads_all[me] = jnp.where(valid, cotangent[...], 0.0).astype(jnp.bfloat16)
    route = [routes[choice : choice + 1, :] for choice in range(2)]
    place = [places[choice : choice + 1, :].astype(jnp.float32) for choice in range(2)]
    meta_send[...] = jnp.zeros_like(meta_send)
    for member in range(members):
        named = [chosen == member for chosen in route]
        meta_send[member, 0:1, :] = jnp.where(
            named[0], place[0], jnp.where(named[1], place[1], -1.0)
        )
        meta_send[member, 1:2, :] = jnp.where(
            named[0], gates[0:1, :], jnp.where(named[1], gates[1:2, :], 0.0)
        )
    meta_all[me] = meta_send[me]
    grad_moves = [
        [
            links.copy(grads_all.at[me], grads_all.at[me], {"exp": peer}),
            links.copy(meta_send.at[peer], meta_all.at[me], {"exp": peer}),
        ]
        for peer in at.peers
    ]
    while len(passed) < groups:
        onward()
    total_gain = gain_ring[0]
    for group in range(1, groups):
        total_gain = total_gain + gain_ring[group]
    gains_full[...] = total_gain.astype(jnp.bfloat16).astype(jnp.float32)
    stream = tokens[...].astype(jnp.float32)
    first_input = (stream * rms_factor(stream) * gains_full[0:1, :]).astype(jnp.bfloat16)
    saved[4] = first_input
    for moves in crossed:
        moves[1].wait_recv()
    for move in passed:
        move.wait_recv()
    tick(5)
    hand_out(attend_full, attend_out)

    cosines, sines = cos_ref[...], sin_ref[...]
    for matrix in range(3):
        raw = matmul(first_input, attend_full[matrix])
        if matrix == 2:
            saved[2] = raw.astype(jnp.bfloat16)
        else:
            for start in range(0, width, 128):
                piece = raw[:, start : start + 128]
                saved[matrix, :, start : start + 128] = (
                    piece * cosines + turned(piece) * sines
                ).astype(jnp.bfloat16)
    tick(6)

    seq_length = length_ref[me]
    rows_at = lax.broadcasted_iota(jnp.int32, (length, length), 0)
    cols_at = lax.broadcasted_iota(jnp.int32, (length, length), 1)
    allowed = (cols_at <= rows_at) & (cols_at < seq_length)
    lower = first_half((length, 128))

    def heads(pair, carry):
        lanes = pl.ds(pl.multiple_of(pair * 128, 128), 128)
        query, key, value = saved[0, :, lanes], saved[1, :, lanes], saved[2, :, lanes]
        results = []
        for side in range(2):
            alone = jnp.where(lower == (side == 0), query, jnp.zeros_like(query))
            scores = jnp.where(allowed, nt(alone, key) * 0.125, -1e30)
            expo = jnp.exp(scores - jnp.max(scores, axis=-1, keepdims=True))
            soft = expo / jnp.sum(expo, axis=-1, keepdims=True)
            soft_ref[2 * pair + side] = soft
            results.append(matmul(soft.astype(jnp.bfloat16), value))
        saved[3, :, lanes] = jnp.where(lower, results[0], results[1]).astype(jnp.bfloat16)
        return carry

    lax.fori_loop(0, width // 128, heads, 0)
    hand_out(saved, saved_out)
    hand_out(soft_ref, soft_out)
    middle = tokens[...].astype(jnp.float32) + matmul(saved[3], attend_full[3])
    middle_ref[...] = middle
    hand_out(middle_ref, middle_out)
    second_all[me] = (middle * rms_factor(middle) * gains_full[1:2, :]).astype(jnp.bfloat16)
    second_moves = [
        links.copy(second_all.at[me], second_all.at[me], {"exp": peer}) for peer in at.peers
    ]
    for moves in grad_moves:
        for move in moves:
            move.wait_recv()
    grads_home[...] = grads_all[slot_of(deal_ref, me)]
    hand_out(grads_home, grads_out)
    tick(7)

    def hits(slot, by_row):
        line = meta_all[slot, 0:1, :]
        if by_row:
            names = lax.broadcasted_iota(jnp.int32, (capacity, length), 0).astype(jnp.float32)
            hit = names == line
        else:
            names = lax.broadcasted_iota(jnp.int32, (length, capacity), 1).astype(jnp.float32)
            hit = names == upright(line)
        return jnp.where(hit, 1.0, 0.0).astype(jnp.bfloat16)

    def spot_of(slot):
        return slice(slot * capacity, (slot + 1) * capacity)

    def here_of(slot):
        return slice(slot * length, (slot + 1) * length)

    for slot in range(members):
        pick = hits(slot, True)
        gate = jnp.sum(pick.astype(jnp.float32) * meta_all[slot, 1:2, :], axis=1, keepdims=True)
        rows_grad[spot_of(slot), :] = (matmul(pick, grads_all[slot]) * gate).astype(jnp.bfloat16)
    for move in second_moves:
        move.wait_recv()
    for slot in range(members):
        inputs_ref[here_of(slot), :] = second_all[deal_ref[slot]]
        rows_in[spot_of(slot), :] = matmul(hits(slot, True), inputs_ref[here_of(slot), :]).astype(
            jnp.bfloat16
        )
    inputs_turned[...] = inputs_ref[...].T
    rows_turned[...] = rows_in[...].T
    dense_out[...] = jnp.zeros_like(dense_out)
    dense_back[...] = jnp.zeros_like(dense_back)
    rows_out[...] = jnp.zeros_like(rows_out)
    rows_back[...] = jnp.zeros_like(rows_back)

    def branch(chunk, inputs, turned_inputs, outer, out, back):
        for step in range(steps):
            for side in range(2):
                for piece in range(2):
                    ring_copy(chunk, step, side, piece).wait_send()

        def part(index, carry):
            lanes = pl.ds(pl.multiple_of(index * 256, 256), 256)
            gate = matmul(inputs[...], wide_full[chunk, 0, :, lanes])
            up = matmul(inputs[...], wide_full[chunk, 1, :, lanes])
            rise = sigmoid(gate)
            smooth = gate * rise
            hidden = (smooth * up).astype(jnp.bfloat16)
            hidden_grad = nt(outer[...], down_full[chunk, lanes, :])
            gate_grad = (hidden_grad * up * (rise * (1.0 + gate * (1.0 - rise)))).astype(
                jnp.bfloat16
            )
            up_grad = (hidden_grad * smooth).astype(jnp.bfloat16)
            out[...] += matmul(hidden, down_full[chunk, lanes, :])
            back[...] += nt(gate_grad, wide_full[chunk, 0, :, lanes]) + nt(
                up_grad, wide_full[chunk, 1, :, lanes]
            )
            down_full[chunk, lanes, :] = tn(hidden, outer[...]).astype(jnp.bfloat16)
            wide_full[chunk, 0, :, lanes] = matmul(turned_inputs[...], gate_grad).astype(
                jnp.bfloat16
            )
            wide_full[chunk, 1, :, lanes] = matmul(turned_inputs[...], up_grad).astype(
                jnp.bfloat16
            )

            @pl.when(index == 0)
            def _():
                for ahead in range(groups // 2):
                    @pl.when(chunk + 1 + ahead < chunks)
                    def _():
                        ring_step(chunk + 1 + ahead, steps - 1 - 2 * ahead)

            return carry

        lax.fori_loop(0, down_full.shape[1] // 256, part, 0)
        kept(chunk, 0).start(priority=1)
        kept(chunk, 1).start(priority=1)

    def kept(chunk, piece):
        source, target = ((wide_full, wide_grads), (down_full, down_grads))[piece]
        return pltpu.make_async_copy(
            source.at[chunk], target.at[chunk], local_sems.at[2 * chunk + piece]
        )

    outer_all = grads_all.reshape(members * length, width)
    flat = (members * length, width)
    dense = (
        inputs_ref,
        inputs_turned,
        outer_all,
        dense_out.reshape(flat),
        dense_back.reshape(flat),
    )

    def first_sum(chunk, side, piece):
        owner = at.owner(-1 if side == 0 else 1)
        if piece == 0:
            spot = wide_full.at[chunk, side, rows(owner * block, block), :]
        else:
            spot = down_full.at[chunk, rows(owner * low + side * (low // 2), low // 2), :]
        return remote(
            spot,
            (wide_first, down_first)[piece].at[chunk, side],
            first_sends,
            first_arrivals,
            chunk * 4 + side * 2 + piece,
            (at.next, at.back)[side],
        )

    early = chunks - 2

    def start_sums(chunk):
        for piece in range(2):
            for side in range(2):
                first_sum(chunk, side, piece).start()

    def next_chunk(chunk, carry):
        for ahead in range(groups // 2):
            @pl.when((chunk > 0) & (chunk + ahead < chunks))
            def _():
                ring_step(chunk + ahead, steps - 2 * ahead)

        @pl.when(chunk == chunks - 1)
        def _():
            for before in range(early):
                start_sums(before)

        @pl.when(chunk == 1)
        def _():
            branch(chunk, *dense)

        @pl.when(chunk != 1)
        def _():
            branch(chunk, rows_in, rows_turned, rows_grad, rows_out, rows_back)

        return carry

    lax.fori_loop(0, chunks, next_chunk, 0)

    for slot in range(members):
        inner = rows_back[spot_of(slot), :].astype(jnp.bfloat16)
        dense_back[slot] += matmul(hits(slot, False), inner)
    for member in range(members):
        back_ref[member] = dense_back[slot_of(deal_ref, member)].astype(jnp.bfloat16)
        hand_out(back_ref.at[member], back_out.at[member])
    for slot in range(members):
        gate = upright(meta_all[slot, 1:2, :])
        picked = matmul(hits(slot, False), rows_out[spot_of(slot), :].astype(jnp.bfloat16))
        dense_out[slot] += gate * picked
        score = jnp.sum(picked * grads_all[slot].astype(jnp.float32), axis=1, keepdims=True)
        gate_ref[slot] = jnp.broadcast_to(lying(score), gate_ref.shape[1:])
    for member in range(members):
        result_ref[member] = dense_out[slot_of(deal_ref, member)].astype(jnp.bfloat16)
        hand_out(result_ref.at[member], result_out.at[member])
    for chunk in range(chunks):
        kept(chunk, 0).wait()
        kept(chunk, 1).wait()
    for chunk in range(early):
        for piece in range(2):
            for side in range(2):
                first_sum(chunk, side, piece).wait()
    for made in outgoing:
        made.wait()
    links.finish()


def scatter_kernel(
    groups,
    members,
    tokens,
    routes,
    gains_full,
    cos_ref,
    sin_ref,
    gate_parts,
    result_parts,
    back_parts,
    wide_grads,
    down_grads,
    wide_first,
    down_first,
    grads_in,
    middle_in,
    attend_in,
    saved_in,
    soft_in,
    output_out,
    input_grad_out,
    expand_out,
    reduce_out,
    narrow_out,
    project_out,
    collect_out,
    gate_grad_ref,
    widen_sum,
    gains_sum,
    expand_sum,
    reduce_sum,
    narrow_sum,
    output_ref,
    input_grad_ref,
    attend_sum,
    grads_home,
    middle_ref,
    attend_full,
    saved,
    soft_ref,
    gate_recv,
    result_recv,
    back_recv,
    wide_own,
    down_own,
    wide_recv,
    down_recv,
    wide_sum,
    turned_ref,
    attend_grad,
    near_recv,
    far_recv,
    far_send,
    attend_total,
    attend_recv,
    attend_back,
    widen_back,
    widen_home,
    gain_own,
    gain_recv,
    gain_ring,
    sends,
    arrivals,
    local_sems,
):
    at = Places(groups, members)
    links = Links(sends, arrivals)
    at.enter()
    me, steps = at.member, groups - 1
    length, width = tokens.shape
    chunks, low = down_own.shape[0], narrow_sum.shape[0]
    share = attend_sum.shape[1]
    block = share * members

    moves_of = {}
    widen_moves = []

    def ring_step(chunk, step):
        made = []
        owners = (at.owner(-1 - step), at.owner(1 + step))
        for piece in range(2):
            for side, target in enumerate((at.next, at.back)):
                own = (wide_own, down_own)[piece]
                landing = (wide_recv, down_recv)[piece].at[chunk, side]
                if piece == 0:
                    spot = (chunk, side, rows(owners[side] * block, block))
                else:
                    spot = (chunk, rows(owners[side] * low + side * (low // 2), low // 2))
                if step == 0:
                    first = (wide_grads, down_grads)[piece]
                    made.append(links.copy(first.at[spot], landing.at[0], target))
                    continue
                if step > 1 or chunk >= early:
                    moves_of[chunk, step - 1][2 * piece + side].wait_recv()
                source = landing.at[step - 1]
                added = source[...].astype(jnp.float32) + own[spot].astype(jnp.float32)
                if step < steps:
                    source[...] = added.astype(jnp.bfloat16)
                elif piece == 0 and chunk != 1:
                    wide_sum[max(chunk - 1, 0), side] = added
                elif piece == 0:
                    for member in range(members):
                        widen_back[member, side] = added[member * share : (member + 1) * share, :]
                else:
                    start = side * (low // 2)
                    if chunk != 1:
                        start = start + max(chunk - 1, 0) * low
                        reduce_sum[start : start + low // 2, :] = added
                    else:
                        narrow_sum[start : start + low // 2, :] = added
                if step < steps:
                    made.append(links.copy(source, landing.at[step], target))
        moves_of[chunk, step] = made
        if step == steps and chunk == 1:
            widen_home[me] = widen_back[me]
            for peer in at.peers:
                widen_moves.append(
                    links.copy(widen_back.at[peer], widen_home.at[me], {"exp": peer})
                )
        if step == steps and chunk == 1:
            store(narrow_sum, narrow_out)
        elif step == steps:
            spot = rows(max(chunk - 1, 0) * low, low)
            store(reduce_sum.at[spot], reduce_out.at[spot])
        if step == steps and chunk and chunk % 2 == 0:
            pair = chunk // 2 - 1
            for side in range(2):
                found = joined_lanes(wide_sum[chunk - 2, side], wide_sum[chunk - 1, side])
                for index in range(0, len(found), 1):
                    expand_sum[pair, side, :, index * 128 : index * 128 + 128] = found[index]
            store(expand_sum.at[pair], expand_out.at[pair])

    early = chunks - 2
    order = [(chunk, 0) for chunk in range(early, chunks)] + [
        (chunk, step) for step in range(1, groups) for chunk in (1, 0, *range(2, chunks))
    ]

    def poll(count):
        for _ in range(min(count, len(order))):
            chunk, step = order.pop(0)
            for made in own_loads.pop(step, ()):
                made.wait()
            ring_step(chunk, step)

    kept, stored = [], []

    def store(source, target):
        made = pltpu.make_async_copy(source, target, local_sems.at[4 * groups + 14 + len(stored)])
        made.start(priority=1)
        stored.append(made)

    def load(source, target):
        made = pltpu.make_async_copy(source, target, local_sems.at[len(kept)])
        made.start(priority=1)
        kept.append(made)
        return made

    own_loads = {}

    def load_own(step):
        found = []
        for side, owner in enumerate((at.owner(-1 - step), at.owner(1 + step))):
            spot = rows(owner * block, block)
            found.append(load(wide_grads.at[:, side, spot], wide_own.at[:, side, spot]))
            spot = rows(owner * low + side * (low // 2), low // 2)
            found.append(load(down_grads.at[:, spot], down_own.at[:, spot]))
        own_loads[step] = found

    back_moves = [
        links.copy(back_parts.at[peer], back_recv.at[me], {"exp": peer}) for peer in at.peers
    ]
    first_loads = [
        load(wide_first.at[:, side], wide_recv.at[0:early, side, 0]) for side in range(2)
    ] + [load(down_first.at[:, side], down_recv.at[0:early, side, 0]) for side in range(2)]
    load_own(1)
    poll(2)
    middle_loads = [
        load(back_parts.at[me], back_recv.at[me]),
        load(middle_in, middle_ref),
        load(grads_in, grads_home),
        load(attend_in.at[3], attend_full.at[3]),
        load(saved_in, saved),
    ]
    soft_load = load(soft_in, soft_ref)
    load_own(2)
    attend_load = load(attend_in.at[0:3], attend_full.at[0:3])
    for step in range(3, groups):
        load_own(step)
    result_load = load(result_parts.at[me], result_recv.at[me])
    gate_recv[me] = gate_parts[me]
    for made in first_loads:
        made.wait()
    poll(3)
    result_moves = [
        [
            links.copy(result_parts.at[peer], result_recv.at[me], {"exp": peer}),
            links.copy(gate_parts.at[peer], gate_recv.at[me], {"exp": peer}),
        ]
        for peer in at.peers
    ]
    for made in middle_loads:
        made.wait()
    for move in back_moves:
        move.wait_recv()

    second_grad = back_recv[0].astype(jnp.float32)
    for member in range(1, members):
        second_grad = second_grad + back_recv[member].astype(jnp.float32)
    middle = middle_ref[...]
    scale = rms_factor(middle)
    gain_own[...] = jnp.zeros_like(gain_own)
    gain_own[1:2, :] = jnp.sum(second_grad * (middle * scale), axis=0, keepdims=True)
    input_grad_ref[...] = grads_home[...].astype(jnp.float32) + rms_back(
        middle, scale, second_grad * gains_full[1:2, :]
    )
    middle_low = input_grad_ref[...].astype(jnp.bfloat16)
    turned_ref[3] = nt(middle_low, attend_full[3]).astype(jnp.bfloat16)
    poll(2)
    cosines, sines = cos_ref[...], sin_ref[...]
    lower = first_half((length, 128))
    soft_load.wait()

    def heads(pair, carry):
        lanes = pl.ds(pl.multiple_of(pair * 128, 128), 128)
        query, key, value = saved[0, :, lanes], saved[1, :, lanes], saved[2, :, lanes]
        outer = turned_ref[3, :, lanes]
        made = []
        for side in range(2):
            soft = soft_ref[2 * pair + side]
            alone = jnp.where(lower == (side == 0), outer, jnp.zeros_like(outer))
            value_grad = tn(soft.astype(jnp.bfloat16), outer)
            soft_grad = nt(alone, value)
            score_grad = (
                soft * (soft_grad - jnp.sum(soft * soft_grad, axis=-1, keepdims=True))
            ).astype(jnp.bfloat16)
            made.append(
                (matmul(score_grad, key) * 0.125, tn(score_grad, query) * 0.125, value_grad)
            )
        for index in range(3):
            joined = jnp.where(lower, made[0][index], made[1][index])
            if index < 2:
                joined = joined * cosines - turned(joined) * sines
            turned_ref[index, :, lanes] = joined.astype(jnp.bfloat16)
        return carry

    attend_grad[3] = tn(saved[3], middle_low).astype(jnp.bfloat16)
    for third in range(3):
        lax.fori_loop(2 * third, 2 * third + 2, heads, 0)
        poll(2)
    for matrix in range(3):
        attend_grad[matrix] = tn(saved[4], turned_ref[matrix]).astype(jnp.bfloat16)
    near_moves = [
        links.copy(attend_grad.at[matrix], near_recv.at[index], {"exp": at.near})
        for index, matrix in enumerate((at.near, at.cross))
    ]
    poll(1)
    attend_load.wait()
    first_grad = nt(turned_ref[0], attend_full[0])
    for matrix in range(1, 3):
        first_grad = first_grad + nt(turned_ref[matrix], attend_full[matrix])
    stream = tokens[...].astype(jnp.float32)
    scale = rms_factor(stream)
    gain_own[0:1, :] = jnp.sum(first_grad * (stream * scale), axis=0, keepdims=True)
    gain_moves = [links.copy(gain_own, gain_recv.at[me], {"exp": peer}) for peer in at.peers]
    gain_recv[me] = gain_own[...]
    input_grad_ref[...] += rms_back(stream, scale, first_grad * gains_full[0:1, :])
    store(input_grad_ref, input_grad_out)
    for move in near_moves:
        move.wait_recv()
    far_send[...] = (
        attend_grad[at.far].astype(jnp.float32) + near_recv[1].astype(jnp.float32)
    ).astype(jnp.bfloat16)
    far_move = links.copy(far_send, far_recv, {"exp": at.far})
    poll(2)
    for moves in result_moves:
        for move in moves:
            move.wait_recv()
    result_load.wait()
    output = middle_ref[...]
    for member in range(members):
        output = output + result_recv[member].astype(jnp.float32)
    output_ref[...] = output
    store(output_ref, output_out)
    for choice in range(2):
        route = routes[choice : choice + 1, :]
        found = jnp.zeros((1, length), jnp.float32)
        for member in range(members):
            found = jnp.where(route == member, gate_recv[member, 0:1, :], found)
        gate_grad_ref[choice : choice + 1, :] = found
    poll(7)
    for move in gain_moves:
        move.wait_recv()
    total = gain_recv[0]
    for member in range(1, members):
        total = total + gain_recv[member]
    gain_ring[at.group] = total
    far_move.wait_recv()
    attend_total[...] = (
        attend_grad[me].astype(jnp.float32)
        + near_recv[0].astype(jnp.float32)
        + far_recv[...].astype(jnp.float32)
    ).astype(jnp.bfloat16)

    reach = (groups // 2, groups - 1 - groups // 2)
    small = {}

    def advance_small(step):
        for side, target in enumerate((at.next, at.back)):
            if step > reach[side]:
                continue
            owner = at.owner(reach[side] - step if side == 0 else step - reach[side])
            spot = attend_total.at[rows(owner * block, block), :]
            if step:
                for move in small[step - 1, side]:
                    move.wait_recv()
            if step < reach[side]:
                source = spot
                if step:
                    source = attend_recv.at[side, step - 1]
                    source[...] = (
                        source[...].astype(jnp.float32) + spot[...].astype(jnp.float32)
                    ).astype(jnp.bfloat16)
                line = gain_ring.at[at.owner(-step if side == 0 else step)]
                small[step, side] = (
                    links.copy(source, attend_recv.at[side, step], target),
                    links.copy(line, line, target),
                )

    for step in range(reach[0] + 1):
        advance_small(step)
        poll(2)
    added = attend_total[rows(at.group * block, block), :].astype(jnp.float32)
    for side in range(2):
        added = added + attend_recv[side, reach[side] - 1].astype(jnp.float32)
    for member in range(members):
        attend_back[member] = added[member * share : (member + 1) * share, :]
    attend_moves = [
        links.copy(attend_back.at[peer], attend_sum.at[me], {"exp": peer}) for peer in at.peers
    ]
    attend_sum[me] = attend_back[me]
    total = gain_ring[0]
    for group in range(1, groups):
        total = total + gain_ring[group]
    count = gains_sum.shape[1]
    start = (at.group * members + me) * count
    gains_sum[...] = pltpu.roll(total, width - start, 1)[0:2, 0:count]
    poll(len(order) - 2)
    for move in attend_moves:
        move.wait_recv()
    store(attend_sum.at[0:3], project_out)
    store(attend_sum.at[3], collect_out)
    for move in widen_moves:
        move.wait_recv()
    for matrix in range(2):
        for member in range(0, members, 2):
            found = joined_lanes(widen_home[member, matrix], widen_home[member + 1, matrix])
            for index, part in enumerate(found):
                start = index * 64 * members + member * 64
                widen_sum[matrix, :, start : start + 128] = part
    poll(len(order))
    for made in stored:
        made.wait()
    links.finish()


def update_kernel(rates, fixed, copies, *refs):
    count = len(rates)
    given, made = refs[: 4 * count + copies], refs[4 * count + copies :]
    for index in range(copies):
        made[index][...] = given[4 * count + index][...]

    def update(index):
        weight, moment, variance, gradient = given[4 * index : 4 * index + 4]
        if len(gradient.shape) > len(weight.shape):
            grad = jnp.concatenate(
                [
                    gradient[at % 2, :, :, at // 2 * 128 : at // 2 * 128 + 128]
                    for at in range(weight.shape[-1] // 128)
                ],
                axis=2,
            )
        else:
            grad = gradient[...]
        grad = 0.5 * grad
        level = 1.0 / (1.0 - 0.5**STEP)
        moment_new = 0.5 * moment[...] + grad
        variance_new = 0.5 * variance[...] + 2.0 * grad * grad
        kept = weight[...]
        stepped = moment_new * level / (jnp.sqrt(variance_new * level) + 1e-08) + 0.1 * kept
        made[copies + 3 * index][...] = moment_new
        made[copies + 3 * index + 1][...] = variance_new
        made[copies + 3 * index + 2][...] = kept - rates[index] * stepped

    for index in range(count):
        if fixed[index]:
            pl.when(pl.program_id(0) == 0)(functools.partial(update, index))
        else:
            update(index)


def update_all(*groups, passed):
    cuts = 4

    def spec(dims, cut):
        if cut is None:
            return pl.BlockSpec(dims, lambda step: (0,) * len(dims))
        block = tuple(size // cuts if at == cut else size for at, size in enumerate(dims))
        return pl.BlockSpec(
            block, lambda step: tuple(step if at == cut else 0 for at in range(len(dims)))
        )

    def cut_of(array):
        dims = array.shape
        for at in range(len(dims) - 1):
            if array.size > 100000 and dims[at] % (8 * cuts) == 0:
                return at
        return len(dims) - 1 if dims[-1] % (128 * cuts) == 0 else None

    given, specs, shapes, out_specs = [], [], [], []
    for _, weight, moment, variance, gradient in groups:
        cut = cut_of(weight)
        for array in (weight, moment, variance, gradient):
            given.append(array)
            more = array.ndim - weight.ndim
            specs.append(spec(array.shape, None if cut is None else cut + more))
        for array in (weight, moment, variance):
            shapes.append(jax.ShapeDtypeStruct(array.shape, array.dtype))
            out_specs.append(spec(array.shape, cut))
    extra = [spec(array.shape, cut_of(array)) for array in passed]
    return pl.pallas_call(
        functools.partial(
            update_kernel,
            [group[0] for group in groups],
            [cut_of(group[1]) is None for group in groups],
            len(passed),
        ),
        grid=(cuts,),
        out_shape=[jax.ShapeDtypeStruct(array.shape, array.dtype) for array in passed] + shapes,
        in_specs=specs + extra,
        out_specs=extra + out_specs,
        compiler_params=pltpu.CompilerParams(vmem_limit_bytes=LIMIT),
    )(*given, *passed)


def rotary_lines(length):
    half = HEAD_FEATURES // 2
    freqs = np.exp(-np.log(10000.0) * np.arange(half) / half)
    angles = np.arange(length)[:, None] * freqs[None, :]
    cosines, sines = np.cos(angles), np.sin(angles)
    return (
        np.concatenate([cosines] * 4, axis=1).astype(np.float32),
        np.concatenate([-sines, sines] * 2, axis=1).astype(np.float32),
    )


def spaces(*names):
    kinds = {"v": pltpu.VMEM, "s": pltpu.SMEM, "a": pl.ANY}
    return [pl.BlockSpec(memory_space=kinds[name]) for name in "".join(names)]


def local(
    tokens,
    seq_lengths,
    deal_order,
    expert_routes,
    capacity_slots,
    gate_weights,
    cotangent,
    projector,
    projector_mean,
    projector_square,
    collector,
    collector_first_moment,
    collector_second_moment,
    widener,
    widener_mean,
    widener_square,
    narrower,
    narrower_mean,
    narrower_square,
    norm_gains,
    gains_mean,
    gains_square,
    expander,
    expander_mean,
    expander_square,
    reducer,
    reducer_mean,
    reducer_square,
):
    groups, members = lax.axis_size("grp"), lax.axis_size("exp")
    length, width = tokens.shape[1:]
    inner = expander.shape[3]
    piece = widener.shape[2] // members
    chunks = 1 + inner // piece
    capacity = 3 * length // members
    steps = groups - 1
    high, low, share = expander.shape[2], narrower.shape[0], projector.shape[1]
    bf16, f32 = jnp.bfloat16, jnp.float32
    shape = jax.ShapeDtypeStruct
    cosines, sines = (jnp.asarray(lines) for lines in rotary_lines(length))
    count = 16 * groups
    (
        wide_grads,
        down_grads,
        wide_first,
        down_first,
        attend_full,
        grads_all,
        saved,
        middle,
        soft,
        result_parts,
        back_parts,
        gains_full,
        gate_parts,
    ) = pl.pallas_call(
        functools.partial(gather_kernel, groups, members),
        out_shape=[
            shape((chunks, 2, width, piece), bf16),
            shape((chunks, piece, width), bf16),
            shape((chunks - 2, 2, high, piece), bf16),
            shape((chunks - 2, 2, low // 2, width), bf16),
            shape((4, width, width), bf16),
            shape((length, width), bf16),
            shape((5, length, width), bf16),
            shape((length, width), f32),
            shape((HEAD_COUNT, length, length), f32),
            shape((members, length, width), bf16),
            shape((members, length, width), bf16),
            shape((8, width), f32),
            shape((members, 8, length), f32),
        ],
        in_specs=spaces("ssvavvvvvvaaaavv"),
        out_specs=spaces("a" * 11, "vv"),
        scratch_shapes=[
            VMEM((length, width), f32),
            VMEM(widener.shape, f32),
            VMEM(narrower.shape, f32),
            VMEM(expander.shape[1:], f32),
            VMEM(reducer.shape[1:], f32),
            VMEM((members, length, width), bf16),
            VMEM((members, length, width), bf16),
            VMEM((length, width), bf16),
            VMEM((4, width, width), bf16),
            VMEM((members, length, width), bf16),
            VMEM((5, length, width), bf16),
            VMEM((length, width), f32),
            VMEM((HEAD_COUNT, length, length), f32),
            VMEM((members, length, width), bf16),
            VMEM((members, 8, length), f32),
            VMEM((members, 8, length), f32),
            VMEM((4, share, width), f32),
            VMEM((4, share, width), f32),
            VMEM((members, 2, share, piece), f32),
            VMEM((members, 2, share, piece), f32),
            VMEM((8, width), f32),
            VMEM((members, 8, width), f32),
            VMEM((groups, 8, width), f32),
            VMEM((chunks, 2, width, piece), bf16),
            VMEM((chunks, piece, width), bf16),
            VMEM((chunks, 2, high, piece), bf16),
            VMEM((chunks, low, width), bf16),
            VMEM((members * length, width), bf16),
            VMEM((width, members * length), bf16),
            VMEM((members, length, width), f32),
            VMEM((members, length, width), f32),
            VMEM((members * capacity, width), bf16),
            VMEM((width, members * capacity), bf16),
            VMEM((members * capacity, width), bf16),
            VMEM((members * capacity, width), f32),
            VMEM((members * capacity, width), f32),
            pltpu.SemaphoreType.DMA((count,)),
            pltpu.SemaphoreType.DMA((count,)),
            pltpu.SemaphoreType.DMA((chunks * steps * 4,)),
            pltpu.SemaphoreType.DMA((chunks * steps * 4,)),
            pltpu.SemaphoreType.DMA((chunks * 4,)),
            pltpu.SemaphoreType.DMA((chunks * 4,)),
            pltpu.SemaphoreType.DMA((2 * chunks + 10 + 2 * members,)),
        ],
        compiler_params=pltpu.CompilerParams(
            collective_id=0, has_side_effects=True, vmem_limit_bytes=LIMIT
        ),
    )(
        seq_lengths,
        deal_order,
        tokens[0],
        cotangent[0],
        expert_routes[0].T,
        capacity_slots[0].T,
        gate_weights[0].T,
        norm_gains,
        projector,
        collector,
        widener,
        narrower,
        expander[0],
        reducer[0],
        cosines,
        sines,
    )
    count = 32 * groups
    (
        output,
        input_grad,
        expand_sum,
        reduce_sum,
        narrow_sum,
        project_sum,
        collect_sum,
        gate_grad,
        widen_sum,
        gains_sum,
    ) = pl.pallas_call(
        functools.partial(scatter_kernel, groups, members),
        out_shape=[
            shape((length, width), f32),
            shape((length, width), f32),
            shape((2, 2, high, inner // 2), f32),
            shape(reducer.shape[1:], f32),
            shape(narrower.shape, f32),
            shape(projector.shape, f32),
            shape(collector.shape, f32),
            shape((2, length), f32),
            shape(widener.shape, f32),
            shape(norm_gains.shape, f32),
        ],
        in_specs=spaces("v" * 6, "a" * 11),
        out_specs=spaces("a" * 7, "vvv"),
        scratch_shapes=[
            VMEM((2, 2, high, inner // 2), f32),
            VMEM(reducer.shape[1:], f32),
            VMEM(narrower.shape, f32),
            VMEM((length, width), f32),
            VMEM((length, width), f32),
            VMEM((4, share, width), f32),
            VMEM((length, width), bf16),
            VMEM((length, width), f32),
            VMEM((4, width, width), bf16),
            VMEM((5, length, width), bf16),
            VMEM((HEAD_COUNT, length, length), f32),
            VMEM((members, 8, length), f32),
            VMEM((members, length, width), bf16),
            VMEM((members, length, width), bf16),
            VMEM((chunks, 2, width, piece), bf16),
            VMEM((chunks, piece, width), bf16),
            VMEM((chunks, 2, steps, high, piece), bf16),
            VMEM((chunks, 2, steps, low // 2, width), bf16),
            VMEM((chunks - 1, 2, high, piece), f32),
            VMEM((4, length, width), bf16),
            VMEM((4, width, width), bf16),
            VMEM((2, width, width), bf16),
            VMEM((width, width), bf16),
            VMEM((width, width), bf16),
            VMEM((width, width), bf16),
            VMEM((2, groups // 2, high, width), bf16),
            VMEM((4, share, width), f32),
            VMEM((members, 2, share, piece), f32),
            VMEM((members, 2, share, piece), f32),
            VMEM((8, width), f32),
            VMEM((members, 8, width), f32),
            VMEM((groups, 8, width), f32),
            pltpu.SemaphoreType.DMA((count,)),
            pltpu.SemaphoreType.DMA((count,)),
            pltpu.SemaphoreType.DMA((4 * groups + 32,)),
        ],
        compiler_params=pltpu.CompilerParams(
            collective_id=1, has_side_effects=True, vmem_limit_bytes=LIMIT
        ),
    )(
        tokens[0],
        expert_routes[0].T,
        gains_full,
        cosines,
        sines,
        gate_parts,
        result_parts,
        back_parts,
        wide_grads,
        down_grads,
        wide_first,
        down_first,
        grads_all,
        middle,
        attend_full,
        saved,
        soft,
    )
    updated = update_all(
        (0.1, projector, projector_mean, projector_square, project_sum),
        (0.3, collector, collector_first_moment, collector_second_moment, collect_sum),
        (0.07, widener, widener_mean, widener_square, widen_sum),
        (0.045, narrower, narrower_mean, narrower_square, narrow_sum),
        (0.2, norm_gains, gains_mean, gains_square, gains_sum),
        (0.07, expander[0], expander_mean[0], expander_square[0], expand_sum),
        (0.045, reducer[0], reducer_mean[0], reducer_square[0], reduce_sum),
        passed=(output, input_grad),
    )
    return (
        updated[0][None],
        updated[1][None],
        gate_grad.T[None],
        *updated[2:17],
        *(found[None] for found in updated[17:]),
    )


def fits(mesh):
    groups, members = mesh.shape["grp"], mesh.shape["exp"]
    share = 64 * HEAD_COUNT // (groups * members)
    return members == 4 and groups % 2 == 0 and share % 8 == 0 and share * members // 2 % 16 == 0


def solution(mesh):
    placed = (
        P(("grp", "exp"), None, None),
        P("grp"),
        P("grp"),
        P(("grp", "exp"), None, None),
        P(("grp", "exp"), None, None),
        P(("grp", "exp"), None, None),
        P(("grp", "exp"), None, None),
        P(None, ("grp", "exp"), None),
        P(None, ("grp", "exp"), None),
        P(None, ("grp", "exp"), None),
        P(("grp", "exp"), None),
        P(("grp", "exp"), None),
        P(("grp", "exp"), None),
        P(None, ("grp", "exp"), None),
        P(None, ("grp", "exp"), None),
        P(None, ("grp", "exp"), None),
        P(("grp", "exp"), None),
        P(("grp", "exp"), None),
        P(("grp", "exp"), None),
        P(None, ("grp", "exp")),
        P(None, ("grp", "exp")),
        P(None, ("grp", "exp")),
        P("exp", None, "grp", None),
        P("exp", None, "grp", None),
        P("exp", None, "grp", None),
        P("exp", "grp", None),
        P("exp", "grp", None),
        P("exp", "grp", None),
    )
    return jax.shard_map(
        local if fits(mesh) else local_plain,
        mesh=mesh,
        in_specs=placed,
        out_specs=(
            P(("grp", "exp"), None, None),
            P(("grp", "exp"), None, None),
            P(("grp", "exp"), None, None),
            P(None, ("grp", "exp"), None),
            P(None, ("grp", "exp"), None),
            P(None, ("grp", "exp"), None),
            P(("grp", "exp"), None),
            P(("grp", "exp"), None),
            P(("grp", "exp"), None),
            P(None, ("grp", "exp"), None),
            P(None, ("grp", "exp"), None),
            P(None, ("grp", "exp"), None),
            P(("grp", "exp"), None),
            P(("grp", "exp"), None),
            P(("grp", "exp"), None),
            P(None, ("grp", "exp")),
            P(None, ("grp", "exp")),
            P(None, ("grp", "exp")),
            P("exp", None, "grp", None),
            P("exp", None, "grp", None),
            P("exp", None, "grp", None),
            P("exp", "grp", None),
            P("exp", "grp", None),
            P("exp", "grp", None),
        ),
        check_vma=False,
    )
```

profile of v0, /device:TPU:0, one launch (start us, length us, event | category | flops | bytes accessed | tf_op | source)
XLA Modules:
  0.0 293.1 jit_solution(15004352630544489328)
XLA Ops:
  0.7 151.7 %shard_map.469 = (bf16[5,2,768,512]{3,2,1,0:T(8,128)(2,1)}, bf16[5,512,768]{2,1,0:T(8,128)(2,1)}, bf16[3,2,96,512]{3,2,1,0:T(8,128)(2,1)}, bf16[3,2,32,768]{3,2,...) custom-call(s32[4]{0:T(128)} %length_ref.1, ...), custom_call_target="tpu_custom_call" | custom-call | tf_op jit(solution)/shard_map/pallas_call | solution.py:1539
  152.4 129.6 %shard_map.470 = (f32[192,768]{1,0:T(8,128)}, f32[192,768]{1,0:T(8,128)}, f32[2,2,96,1024]{3,2,1,0:T(8,128)}, f32[256,768]{1,0:T(8,128)}, f32[64,768]{1,0:T(8,12...) custom-call(bf16[192,768]{1,0:T(8,128)(2,1)} %bitcast.35, ...), custom_call_target="tpu_custom_call" | custom-call | tf_op jit(solution)/shard_map/pallas_call | solution.py:1636
  282.0 0.0 copy-start
  282.0 10.5 %shard_map.471 = (f32[192,768]{1,0:T(8,128)}, f32[192,768]{1,0:T(8,128)}, f32[3,24,768]{2,1,0:T(8,128)}, f32[3,24,768]{2,1,0:T(8,128)}, f32[3,24,768]{2,1,0:T(8,...) custom-call(f32[3,24,768]{2,1,0:T(8,128)} %refs_0_.1, ...), custom_call_target="tpu_custom_call" | custom-call | tf_op jit(solution)/shard_map/pallas_call | solution.py:1452
  292.5 0.0 copy-done
  292.5 0.6 copy.55
Async XLA Ops:
  282.0 10.5 %copy-start = (f32[2,192]{1,0:T(2,128)S(1)}, f32[2,192]{1,0:T(2,128)}, u32[]{:S(2)}) copy-start(f32[2,192]{1,0:T(2,128)} %get-tuple-element.94) | copy-start | bytes 4612
where the time goes:
time: 294 us; the launch traced here: 293 us
  Pallas kernels  292 us (99%)
    pallas_call x1, Pallas kernels, local(): pl.pallas_call(functools.partial(gather_kernel, groups, members), out_sha...  152 us
    pallas_call x1, Pallas kernels, local(): pl.pallas_call(functools.partial(scatter_kernel, groups, members), out_sh...  130 us
    pallas_call x1, Pallas kernels, update_all(): pl.pallas_call(functools.partial(update_kernel, [group[0] for group in gr...  10.5 us

commit v1 on v0

--- a/solution.py
+++ b/solution.py
@@ -667,15 +667,6 @@
     ]
     gain_recv[me] = gains[...]
     attend_recv[me] = attend_send[me]
-    loads["widener"].wait()
-    for matrix in range(2):
-        for member in range(members):
-            widen_send[member, matrix] = dealt_lanes(widener[matrix], member, members)
-    widen_moves = [
-        links.copy(widen_send.at[peer], widen_recv.at[me], {"exp": peer}) for peer in at.peers
-    ]
-    widen_recv[me] = widen_send[me]
-
     def stage(chunk):
         if chunk == 1:
             for matrix in range(2):
@@ -694,10 +685,6 @@
             wide_full[chunk, side, rows(at.group * block, block), :] = wide_own[chunk, side]
         down_full[chunk, rows(at.group * low, low), :] = down_own[chunk]
 
-    loads["expander"].wait()
-    loads["reducer"].wait()
-    stage(0)
-    tick(0)
     for moves in first_moves:
         for move in moves:
             move.wait_recv()
@@ -749,6 +736,19 @@
             crossed.append(across(owner))
         for _ in range(waiting):
             onward()
+        if step == 0:
+            loads["expander"].wait()
+            loads["reducer"].wait()
+            stage(0)
+            tick(0)
+            loads["widener"].wait()
+            for matrix in range(2):
+                for member in range(members):
+                    widen_send[member, matrix] = dealt_lanes(widener[matrix], member, members)
+            widen_moves = [
+                links.copy(widen_send.at[peer], widen_recv.at[me], {"exp": peer}) for peer in at.peers
+            ]
+            widen_recv[me] = widen_send[me]
         if step == 1:
             for move in widen_moves:
                 move.wait_recv()
@@ -1237,7 +1237,7 @@
     )
     middle_low = input_grad_ref[...].astype(jnp.bfloat16)
     turned_ref[3] = nt(middle_low, attend_full[3]).astype(jnp.bfloat16)
-    poll(2)
+    poll(3)
     cosines, sines = cos_ref[...], sin_ref[...]
     lower = first_half((length, 128))
     soft_load.wait()
@@ -1268,7 +1268,7 @@
     attend_grad[3] = tn(saved[3], middle_low).astype(jnp.bfloat16)
     for third in range(3):
         lax.fori_loop(2 * third, 2 * third + 2, heads, 0)
-        poll(2)
+        poll(3)
     for matrix in range(3):
         attend_grad[matrix] = tn(saved[4], turned_ref[matrix]).astype(jnp.bfloat16)
     near_moves = [
@@ -1309,7 +1309,7 @@
         for member in range(members):
             found = jnp.where(route == member, gate_recv[member, 0:1, :], found)
         gate_grad_ref[choice : choice + 1, :] = found
-    poll(7)
+    poll(3)
     for move in gain_moves:
         move.wait_recv()
     total = gain_recv[0]

time: 294 us -> 297 us (1.010)
  Pallas kernels: 292 us -> 295 us
    pallas_call x1, Pallas kernels: 152 us -> 155 us  [local(): pl.pallas_call(functools.partial(gather_kernel, groups, members), out_sha...]
where the time goes in v1:
time: 297 us
  Pallas kernels  295 us (99%)
    pallas_call x1, Pallas kernels, local(): pl.pallas_call(functools.partial(gather_kernel, groups, members), out_sha...  155 us
    pallas_call x1, Pallas kernels, local(): pl.pallas_call(functools.partial(scatter_kernel, groups, members), out_sh...  130 us
    pallas_call x1, Pallas kernels, update_all(): pl.pallas_call(functools.partial(update_kernel, [group[0] for group in gr...  10.5 us

profile of v1, /device:TPU:0, one launch (start us, length us, event | category | flops | bytes accessed | tf_op | source)
XLA Modules:
  0.0 296.7 jit_solution(4164194616088862626)
XLA Ops:
  0.7 154.9 %shard_map.469 = (bf16[5,2,768,512]{3,2,1,0:T(8,128)(2,1)}, bf16[5,512,768]{2,1,0:T(8,128)(2,1)}, bf16[3,2,96,512]{3,2,1,0:T(8,128)(2,1)}, bf16[3,2,32,768]{3,2,...) custom-call(s32[4]{0:T(128)} %length_ref.1, ...), custom_call_target="tpu_custom_call" | custom-call | tf_op jit(solution)/shard_map/pallas_call | solution.py:1539
  155.6 130.0 %shard_map.470 = (f32[192,768]{1,0:T(8,128)}, f32[192,768]{1,0:T(8,128)}, f32[2,2,96,1024]{3,2,1,0:T(8,128)}, f32[256,768]{1,0:T(8,128)}, f32[64,768]{1,0:T(8,12...) custom-call(bf16[192,768]{1,0:T(8,128)(2,1)} %bitcast.35, ...), custom_call_target="tpu_custom_call" | custom-call | tf_op jit(solution)/shard_map/pallas_call | solution.py:1636
  285.6 0.0 copy-start
  285.6 10.5 %shard_map.471 = (f32[192,768]{1,0:T(8,128)}, f32[192,768]{1,0:T(8,128)}, f32[3,24,768]{2,1,0:T(8,128)}, f32[3,24,768]{2,1,0:T(8,128)}, f32[3,24,768]{2,1,0:T(8,...) custom-call(f32[3,24,768]{2,1,0:T(8,128)} %refs_0_.1, ...), custom_call_target="tpu_custom_call" | custom-call | tf_op jit(solution)/shard_map/pallas_call | solution.py:1452
  296.1 0.0 copy-done
  296.1 0.6 copy.55
Async XLA Ops:
  285.6 10.5 %copy-start = (f32[2,192]{1,0:T(2,128)S(1)}, f32[2,192]{1,0:T(2,128)}, u32[]{:S(2)}) copy-start(f32[2,192]{1,0:T(2,128)} %get-tuple-element.94) | copy-start | bytes 4612
